TPU v7x, 32 devices: a whole 2x2x4 slice. The times are simulated.
32 devices in a mesh: blk: 8 (over z, x), heads: 4 (over y, core).
Axes of the slice: x: 2, y: 2, z: 4, core: 2. Of those that a mesh axis runs over, the one named last changes fastest.
Arguments:
- queries: float32 [512, 8192], P('blk', 'heads'), may hold values from -6 to 6
- visual_keys: float32 [8192, 1024], P('blk', 'heads'), may hold values from -6 to 6
- projected_values: float32 [8192, 1024], P('blk', 'heads'), may hold values from -6 to 6
- valid_lengths: int32 [8], P('blk'), may hold values from 256 to 1024, as said below
Outputs:
- attended: float32 [512, 8192], P('blk', 'heads')
Inputs may be any that keep to these rules, and one draw needn't show every extreme that they name: `valid_lengths`: some block has all 1024 tokens valid in every draw.
All inputs are finite; a program needn't handle non-finite values.
Results may differ from a plain program's by a relative error of at most 0.0003.
Values sent between devices are 32-bit elements; how exact they have to be, the bound alone decides.
A program may use at most 64 MiB of HBM per device.

v0:
```python
import jax
import jax.numpy as jnp
from jax import lax
from jax.sharding import PartitionSpec as P

HEAD_DIM = 128
SPAN = 6


def passed_along(shard, axis, by):
    size = lax.axis_size(axis)
    return lax.ppermute(shard, axis, [(i, (i + by) % size) for i in range(size)])


def attend(partial_value, query_tile, key_tile, value_tile, usable):
    peak_score, weight_sum, numerator = partial_value
    scores = jnp.einsum("qhgd,khd->hgqk", query_tile, key_tile, precision=lax.Precision.HIGHEST)
    scores = jnp.where(usable, scores, -1e30)
    new_peak = jnp.maximum(peak_score, jnp.max(scores, axis=-1))
    weights = jnp.where(usable, jnp.exp(scores - new_peak[..., None]), 0.0)
    factor = jnp.exp(peak_score - new_peak)
    weight_sum = weight_sum * factor + jnp.sum(weights, axis=-1)
    numerator = numerator * jnp.transpose(factor, (2, 0, 1))[..., None] + jnp.einsum(
        "hgqk,khd->qhgd", weights, value_tile, precision=lax.Precision.HIGHEST
    )
    return (new_peak, weight_sum, numerator)


def combine(upper_part, lower_part):
    new_peak = jnp.maximum(upper_part[0], lower_part[0])
    upper_factor = jnp.exp(upper_part[0] - new_peak)
    lower_factor = jnp.exp(lower_part[0] - new_peak)
    weight_sum = upper_part[1] * upper_factor + lower_part[1] * lower_factor
    numerator = (
        upper_part[2] * jnp.transpose(upper_factor, (2, 0, 1))[..., None]
        + lower_part[2] * jnp.transpose(lower_factor, (2, 0, 1))[..., None]
    )
    return (new_peak, weight_sum, numerator)


def per_device(queries, visual_keys, projected_values, valid_lengths):
    shard_blocks = lax.axis_size("blk")
    window = min(SPAN, shard_blocks // 2)
    left_reach = window // 2 - 1
    right_reach = window // 2
    device_pos = lax.axis_index("blk")
    query_rows = queries.shape[0]
    key_rows = visual_keys.shape[0]
    kv_heads = visual_keys.shape[1] // HEAD_DIM
    group_size = queries.shape[1] // (HEAD_DIM * kv_heads)
    query_tile = (queries * HEAD_DIM ** (-0.5)).reshape(query_rows, kv_heads, group_size, HEAD_DIM)
    key_tile = visual_keys.reshape(key_rows, kv_heads, HEAD_DIM)
    value_tile = projected_values.reshape(key_rows, kv_heads, HEAD_DIM)
    positions = jnp.arange(key_rows, dtype=jnp.int32)
    own_usable = positions < valid_lengths[0]
    initial = (
        jnp.full((kv_heads, group_size, query_rows), -1e30, jnp.float32),
        jnp.zeros((kv_heads, group_size, query_rows), jnp.float32),
        jnp.zeros((query_rows, kv_heads, group_size, HEAD_DIM), jnp.float32),
    )

    def query_usable(offset):
        owner_block = device_pos - offset
        return own_usable & (owner_block >= 0) & (owner_block < shard_blocks)

    upper_state = attend(initial, query_tile, key_tile, value_tile, query_usable(0))

    def climb_up(position, carried):
        arrived = passed_along((carried[0], carried[1], carried[2], carried[3]), "blk", 1)
        outcome = attend(
            (arrived[1], arrived[2], arrived[3]),
            arrived[0],
            key_tile,
            value_tile,
            query_usable(position),
        )
        return (arrived[0],) + outcome

    upper_carried = lax.fori_loop(1, right_reach + 1, climb_up, (query_tile,) + upper_state)
    upper_home = passed_along(
        (upper_carried[1], upper_carried[2], upper_carried[3]), "blk", -right_reach
    )
    lowering = passed_along(query_tile, "blk", -1)
    lower_state = attend(initial, lowering, key_tile, value_tile, query_usable(-1))

    def descend(position, carried):
        arrived = passed_along((carried[0], carried[1], carried[2], carried[3]), "blk", -1)
        outcome = attend(
            (arrived[1], arrived[2], arrived[3]),
            arrived[0],
            key_tile,
            value_tile,
            query_usable(-position),
        )
        return (arrived[0],) + outcome

    lower_carried = lax.fori_loop(2, left_reach + 1, descend, (lowering,) + lower_state)
    lower_home = passed_along(
        (lower_carried[1], lower_carried[2], lower_carried[3]), "blk", left_reach
    )
    final_state = combine(upper_home, lower_home)
    weight_sum = final_state[1]
    numerator = final_state[2]
    normed = numerator / jnp.transpose(weight_sum, (2, 0, 1))[..., None]
    return normed.reshape(query_rows, kv_heads * group_size * HEAD_DIM)


def solution(mesh):
    return jax.shard_map(
        per_device,
        mesh=mesh,
        in_specs=(P("blk", "heads"), P("blk", "heads"), P("blk", "heads"), P("blk")),
        out_specs=P("blk", "heads"),
        check_vma=False,
    )
```

profile of v0, /device:TPU:0, one launch (start us, length us, event | category | flops | bytes accessed | tf_op | source)
XLA Modules:
  0.0 132.5 jit_solution(15396465953049328212)
XLA Ops:
  0.0 1.1 multiply_bitcast_fusion
  1.1 0.1 copy.58
  1.2 0.8 copy.27
  2.0 6.0 %collective-permute-start.6 = (f32[64,2,8,128]{3,2,0,1:T(8,128)}, f32[64,2,8,128]{3,2,0,1:T(8,128)}, u32[]{:S(2)}, u32[]{:S(2)}) collective-permute-start(f32[64,2,8,128]{3,2,0,1:T(8,128)} %copy.27), channel_id=1, source_target_pairs={{0,28},{4,0},{8,4},{12,8},{16,12},{20,16},{24,20},{28,24},{1,29},{... | collective-permute-start | bytes 1572872 | tf_op jit(solution)/shard_map/ppermute | solution.py:12
  8.0 1.0 copy.31
  9.0 1.6 %copy.29 = f32[1024,256]{0,1:T(8,128)S(1)} copy(f32[1024,256]{1,0:T(8,128)} %param.8) | data formatting | bytes 2097152 | tf_op args[2]
  11.2 1.6 %copy.26 = f32[1024,256]{0,1:T(8,128)S(1)} copy(f32[1024,256]{1,0:T(8,128)} %param.7) | data formatting | bytes 2097152 | tf_op args[1]
  12.8 5.1 %bitcast_reduce_fusion.2 = (f32[2,8,64]{1,2,0:T(8,128)S(1)}, f32[2,64,8,1024]{3,2,1,0:T(8,128)}) fusion(pred[1024]{0:T(1024)(128)(4,1)S(1)} %fusion.69, f32[1024,2,128,1]{0,2,3,1:T(8,128)S(1)} %bitcast.126, f32[64,2,8,128]{3,2,1,0:T(8,128)S(1)} %bitcast.131), kind=kOutput, calls=%fused_computation.30 | convolution fusion | flops 1612708864 | bytes 5772288 | tf_op jit(solution)/shard_map/qhgd,khd->hgqk/dot_general | solution.py:17
  17.9 0.1 copy.32
  18.0 3.2 %fusion.33 = f32[2,8,64]{1,2,0:T(8,128)S(1)} fusion(f32[2,64,8,1024]{3,2,1,0:T(8,128)} %get-tuple-element.244, f32[2,8,64]{1,2,0:T(8,128)S(1)} %broadcast_maximum_fusion.1, pred[1024]{0:T(1024)(128)(4,1)S(1)} %fusion.69), kind=kLoop, calls=%fused_computation.34 | loop fusion | flops 4193280 | bytes 4203520 | tf_op jit(solution)/shard_map/reduce_sum | solution.py:22
  21.2 0.1 copy.33
  21.3 5.7 %fusion.53 = f32[64,2,8,128]{3,2,0,1:T(8,128)S(1)} fusion(f32[1024,2,128,1]{0,2,3,1:T(8,128)S(1)} %bitcast.132, f32[2,64,8,1024]{3,2,1,0:T(8,128)} %get-tuple-element.244, f32[2,8,64]{1,2,0:T(8,128)S(1)} %broadcast_maximum_fusion.1, pred[1024]{0:T(1024)(128)(4,1)S(1)} %fusion.69, f32[64,2,8]{2,0,1:T(8,128)S(1)} %get-tuple-element.239), kind=kOutput, calls=%fused_computation.49 | convolution fusion | flops 1613889536 | bytes 5776384 | tf_op jit(solution)/shard_map/hgqk,khd->qhgd/dot_general | solution.py:23
  27.0 0.9 copy.34
  27.9 0.3 copy.35
  28.2 1.3 copy.36
  29.5 67.5 %while.20 = (s32[]{:T(128)}, f32[64,2,8,128]{3,0,2,1:T(8,128)}, f32[2,8,64]{2,1,0:T(8,128)S(1)}, f32[2,8,64]{2,1,0:T(8,128)S(1)}, f32[64,2,8,128]{3,0,2,1:T(8,12...) while((s32[]{:T(128)}, f32[64,2,8,128]{3,0,2,1:T(8,128)}, ...), condition=%wide.region_5.6_spmd.clone, body=%wide.region_2.5_spmd.clone.sunk | while | flops 3230930944 | bytes 25784660 | solution.py:79
  29.5 0.0 collective-permute-start
  29.5 0.0 collective-permute-start.1
  29.5 0.5 collective-permute-start.2
  30.1 2.4 %collective-permute-start.3 = (f32[64,2,8,128]{3,0,2,1:T(8,128)}, f32[64,2,8,128]{3,0,2,1:T(8,128)}, u32[]{:S(2)}, u32[]{:S(2)}) collective-permute-start(f32[64,2,8,128]{3,0,2,1:T(8,128)} %get-tuple-element.324), channel_id=1, source_target_pairs={{0,4},{4,8},{8,12},{12,16},{16,20},{20,24},{24,28},{28,0},{1,5},{5... | collective-permute-start | bytes 1572872 | tf_op jit(solution)/shard_map/while/body/eval_jaxpr/ppermute | solution.py:12
  32.5 0.7 fusion.92
  33.1 14.2 %collective-permute-done = f32[64,2,8,128]{3,0,2,1:T(8,128)S(1)} collective-permute-done((f32[64,2,8,128]{3,0,2,1:T(8,128)}, f32[64,2,8,128]{3,0,2,1:T(8,128)S(1)}, u32[]{:S(2)}, u32[]{:S(2)}) %collective-permute-start) | collective-permute-done | bytes 524320 | tf_op jit(solution)/shard_map/while/body/eval_jaxpr/ppermute | solution.py:12
  47.3 3.8 %bitcast_reduce_fusion.4 = (f32[2,8,64]{2,1,0:T(8,128)S(1)}, f32[2,1024,64,8]{1,2,3,0:T(8,128)S(1)}) fusion(pred[1024]{0:T(1024)(128)(4,1)S(1)} %fusion.92, f32[64,2,8,128]{3,0,2,1:T(8,128)S(1)} %collective-permute-done, f32[1024,2,128]{2,0,1:T(8,128)S(1)} %get-tuple-element.338), kind=kOutput, calls=%fused_computation.2.clone.1 | convolution fusion | flops 1612708864 | bytes 5772288 | tf_op jit(solution)/shard_map/while/body/eval_jaxpr/qhgd,khd->hgqk/dot_general | solution.py:17
  51.1 0.0 collective-permute-done.1
  51.1 1.0 fusion.94
  52.2 0.8 copy.77
  53.0 0.0 collective-permute-done.2
  53.0 4.5 %collective-permute-done.3 = f32[64,2,8,128]{3,0,2,1:T(8,128)} collective-permute-done((f32[64,2,8,128]{3,0,2,1:T(8,128)}, f32[64,2,8,128]{3,0,2,1:T(8,128)}, u32[]{:S(2)}, u32[]{:S(2)}) %collective-permute-start.3) | collective-permute-done | bytes 524320 | tf_op jit(solution)/shard_map/while/body/eval_jaxpr/ppermute | solution.py:12
  57.5 0.0 copy-done.2
  57.5 6.2 %multiply_add_fusion.5 = f32[64,2,8,128]{3,0,2,1:T(8,128)} fusion(f32[64,2,8,128]{3,0,2,1:T(8,128)} %collective-permute-done.3, f32[64,2,8]{0,2,1:T(8,128)S(1)} %get-tuple-element.307, f32[1024,2,128]{2,0,1:T(8,128)S(1)} %copy-done.2, f32[2,1024,64,8]{1,2,3,0:T(8,128)S(1)} %get-tuple-element.306, f32[2,8,64]{2,1,0:T(8,128)S(1)} %get-tuple-element.334, ...), kind=kOutput, calls=%fused_computation.16.clone.1 | convolution fusion | flops 1614020608 | bytes 6300672 | tf_op jit(solution)/shard_map/while/body/eval_jaxpr/hgqk,khd->qhgd/dot_general | solution.py:23
  63.7 0.0 collective-permute-start
  63.7 0.0 collective-permute-start.1
  63.7 0.0 collective-permute-start.2
  63.8 1.1 collective-permute-start.3
  64.9 0.7 fusion.92
  65.5 16.0 %collective-permute-done = f32[64,2,8,128]{3,0,2,1:T(8,128)S(1)} collective-permute-done((f32[64,2,8,128]{3,0,2,1:T(8,128)}, f32[64,2,8,128]{3,0,2,1:T(8,128)S(1)}, u32[]{:S(2)}, u32[]{:S(2)}) %collective-permute-start) | collective-permute-done | bytes 524320 | tf_op jit(solution)/shard_map/while/body/eval_jaxpr/ppermute | solution.py:12
  81.5 3.8 %bitcast_reduce_fusion.4 = (f32[2,8,64]{2,1,0:T(8,128)S(1)}, f32[2,1024,64,8]{1,2,3,0:T(8,128)S(1)}) fusion(pred[1024]{0:T(1024)(128)(4,1)S(1)} %fusion.92, f32[64,2,8,128]{3,0,2,1:T(8,128)S(1)} %collective-permute-done, f32[1024,2,128]{2,0,1:T(8,128)S(1)} %get-tuple-element.338), kind=kOutput, calls=%fused_computation.2.clone.1 | convolution fusion | flops 1612708864 | bytes 5772288 | tf_op jit(solution)/shard_map/while/body/eval_jaxpr/qhgd,khd->hgqk/dot_general | solution.py:17
  85.3 0.0 collective-permute-done.1
  85.4 1.0 fusion.94
  86.4 0.8 copy.77
  87.2 0.0 collective-permute-done.2
  87.2 3.6 %collective-permute-done.3 = f32[64,2,8,128]{3,0,2,1:T(8,128)} collective-permute-done((f32[64,2,8,128]{3,0,2,1:T(8,128)}, f32[64,2,8,128]{3,0,2,1:T(8,128)}, u32[]{:S(2)}, u32[]{:S(2)}) %collective-permute-start.3) | collective-permute-done | bytes 524320 | tf_op jit(solution)/shard_map/while/body/eval_jaxpr/ppermute | solution.py:12
  90.8 6.2 %multiply_add_fusion.5 = f32[64,2,8,128]{3,0,2,1:T(8,128)} fusion(f32[64,2,8,128]{3,0,2,1:T(8,128)} %collective-permute-done.3, f32[64,2,8]{0,2,1:T(8,128)S(1)} %get-tuple-element.307, f32[1024,2,128]{2,0,1:T(8,128)S(1)} %copy-done.2, f32[2,1024,64,8]{1,2,3,0:T(8,128)S(1)} %get-tuple-element.306, f32[2,8,64]{2,1,0:T(8,128)S(1)} %get-tuple-element.334, ...), kind=kOutput, calls=%fused_computation.16.clone.1 | convolution fusion | flops 1614020608 | bytes 6300672 | tf_op jit(solution)/shard_map/while/body/eval_jaxpr/hgqk,khd->qhgd/dot_general | solution.py:23
  97.0 1.3 %copy.37 = f32[64,2,8,128]{3,2,0,1:T(8,128)S(1)} copy(f32[64,2,8,128]{3,0,2,1:T(8,128)} %get-tuple-element.161) | data formatting | bytes 1048576 | tf_op jit(solution)/shard_map/while | solution.py:79
  98.4 0.3 collective-permute-start.4
  98.7 0.0 collective-permute-done.6
  98.7 4.9 %bitcast_reduce_fusion.1 = (f32[2,8,64]{1,2,0:T(8,128)S(1)}, f32[2,64,8,1024]{3,2,1,0:T(8,128)S(1)}) fusion(pred[1024]{0:T(1024)(128)(4,1)S(1)} %fusion.70, f32[64,2,8,128]{3,2,0,1:T(8,128)} %collective-permute-done.6, f32[1024,2,128,1]{0,2,3,1:T(8,128)S(1)} %bitcast.128), kind=kOutput, calls=%fused_computation.26 | convolution fusion | flops 1612708864 | bytes 5772288 | tf_op jit(solution)/shard_map/qhgd,khd->hgqk/dot_general | solution.py:17
  103.6 1.0 fusion.34
  104.7 4.4 %fusion.56 = f32[64,2,8,128]{3,2,0,1:T(8,128)S(1)} fusion(f32[1024,2,128,1]{0,2,3,1:T(8,128)S(1)} %bitcast.134, f32[2,64,8,1024]{3,2,1,0:T(8,128)S(1)} %get-tuple-element.242, f32[2,8,64]{1,2,0:T(8,128)S(1)} %broadcast_maximum_fusion, pred[1024]{0:T(1024)(128)(4,1)S(1)} %fusion.70, f32[64,2,8]{2,0,1:T(8,128)S(1)} %get-tuple-element.238), kind=kOutput, calls=%fused_computation.50 | convolution fusion | flops 1613889536 | bytes 5776384 | tf_op jit(solution)/shard_map/hgqk,khd->qhgd/dot_general | solution.py:23
  109.1 0.1 collective-permute-start.8
  109.3 0.1 copy.38
  109.4 0.1 collective-permute-start.5
  109.5 0.1 copy.42
  109.5 0.1 collective-permute-start.9
  109.6 5.2 %collective-permute-start.7 = (f32[2,8,64]{1,2,0:T(8,128)S(1)}, f32[2,8,64]{1,2,0:T(8,128)S(1)}, u32[]{:S(2)}, u32[]{:S(2)}) collective-permute-start(f32[2,8,64]{1,2,0:T(8,128)S(1)} %broadcast_maximum_fusion), channel_id=1, source_target_pairs={{0,4},{4,8},{8,12},{12,16},{16,20},{20,24},{24,28},{28,0},{1,5},{5... | collective-permute-start | bytes 12296 | tf_op jit(solution)/shard_map/ppermute | solution.py:12
  114.8 0.0 collective-permute-done.5
  114.8 12.2 %collective-permute-start.10 = (f32[2,8,64]{1,2,0:T(8,128)S(1)}, f32[2,8,64]{1,2,0:T(8,128)S(1)}, u32[]{:S(2)}, u32[]{:S(2)}) collective-permute-start(f32[2,8,64]{1,2,0:T(8,128)S(1)} %get-tuple-element.237), channel_id=1, source_target_pairs={{0,4},{4,8},{8,12},{12,16},{16,20},{20,24},{24,28},{28,0},{1,5},{5... | collective-permute-start | bytes 12296 | tf_op jit(solution)/shard_map/ppermute | solution.py:12
  127.1 0.0 collective-permute-done.9
  127.1 1.4 %collective-permute-done.7 = f32[2,8,64]{1,2,0:T(8,128)S(1)} collective-permute-done((f32[2,8,64]{1,2,0:T(8,128)S(1)}, f32[2,8,64]{1,2,0:T(8,128)S(1)}, u32[]{:S(2)}, u32[]{:S(2)}) %collective-permute-start.7) | collective-permute-done | bytes 4128 | tf_op jit(solution)/shard_map/ppermute | solution.py:12
  128.5 2.4 %collective-permute-done.10 = f32[2,8,64]{1,2,0:T(8,128)S(1)} collective-permute-done((f32[2,8,64]{1,2,0:T(8,128)S(1)}, f32[2,8,64]{1,2,0:T(8,128)S(1)}, u32[]{:S(2)}, u32[]{:S(2)}) %collective-permute-start.10) | collective-permute-done | bytes 4128 | tf_op jit(solution)/shard_map/ppermute | solution.py:12
  131.0 0.0 collective-permute-done.4
  131.0 0.0 collective-permute-done.8
  131.0 0.5 add_divide_fusion
  131.5 1.0 copy.65
  (19 shorter events, 0.2 us)
Async XLA Ops:
  2.0 96.7 %collective-permute-start.6 = (f32[64,2,8,128]{3,2,0,1:T(8,128)}, f32[64,2,8,128]{3,2,0,1:T(8,128)}, u32[]{:S(2)}, u32[]{:S(2)}) collective-permute-start(f32[64,2,8,128]{3,2,0,1:T(8,128)} %copy.27), channel_id=1, source_target_pairs={{0,28},{4,0},{8,4},{12,8},{16,12},{20,16},{24,20},{28,24},{1,29},{... | collective-permute-start | bytes 1572872 | tf_op jit(solution)/shard_map/ppermute | solution.py:12
  10.5 17.7 %copy-start = (f32[1024,256]{0,1:T(8,128)}, f32[1024,256]{0,1:T(8,128)S(1)}, u32[]{:S(2)}) copy-start(f32[1024,256]{0,1:T(8,128)S(1)} %copy.29) | copy-start | bytes 3145732
  29.5 17.8 %collective-permute-start = (f32[64,2,8,128]{3,0,2,1:T(8,128)}, f32[64,2,8,128]{3,0,2,1:T(8,128)S(1)}, u32[]{:S(2)}, u32[]{:S(2)}) collective-permute-start(f32[64,2,8,128]{3,0,2,1:T(8,128)} %get-tuple-element.321), channel_id=1, source_target_pairs={{0,4},{4,8},{8,12},{12,16},{16,20},{20,24},{24,28},{28,0},{1,5},{5... | collective-permute-start | bytes 1572872 | tf_op jit(solution)/shard_map/while/body/eval_jaxpr/ppermute | solution.py:12
  29.5 21.6 %collective-permute-start.1 = (f32[2,8,64]{2,1,0:T(8,128)S(1)}, f32[2,8,64]{2,1,0:T(8,128)S(1)}, u32[]{:S(2)}, u32[]{:S(2)}) collective-permute-start(f32[2,8,64]{2,1,0:T(8,128)S(1)} %get-tuple-element.322), channel_id=1, source_target_pairs={{0,4},{4,8},{8,12},{12,16},{16,20},{20,24},{24,28},{28,0},{1,5},{5... | collective-permute-start | bytes 12296 | tf_op jit(solution)/shard_map/while/body/eval_jaxpr/ppermute | solution.py:12
  29.5 23.5 %collective-permute-start.2 = (f32[2,8,64]{2,1,0:T(8,128)S(1)}, f32[2,8,64]{2,1,0:T(8,128)S(1)}, u32[]{:S(2)}, u32[]{:S(2)}) collective-permute-start(f32[2,8,64]{2,1,0:T(8,128)S(1)} %get-tuple-element.323), channel_id=1, source_target_pairs={{0,4},{4,8},{8,12},{12,16},{16,20},{20,24},{24,28},{28,0},{1,5},{5... | collective-permute-start | bytes 12296 | tf_op jit(solution)/shard_map/while/body/eval_jaxpr/ppermute | solution.py:12
  30.1 27.5 %collective-permute-start.3 = (f32[64,2,8,128]{3,0,2,1:T(8,128)}, f32[64,2,8,128]{3,0,2,1:T(8,128)}, u32[]{:S(2)}, u32[]{:S(2)}) collective-permute-start(f32[64,2,8,128]{3,0,2,1:T(8,128)} %get-tuple-element.324), channel_id=1, source_target_pairs={{0,4},{4,8},{8,12},{12,16},{16,20},{20,24},{24,28},{28,0},{1,5},{5... | collective-permute-start | bytes 1572872 | tf_op jit(solution)/shard_map/while/body/eval_jaxpr/ppermute | solution.py:12
  47.3 10.2 %copy-start.2 = (f32[1024,2,128]{2,0,1:T(8,128)S(1)}, f32[1024,2,128]{2,0,1:T(8,128)}, u32[]{:S(2)}) copy-start(f32[1024,2,128]{2,0,1:T(8,128)} %get-tuple-element.339) | copy-start | bytes 3145732 | tf_op jit(solution)/shard_map/while
  63.7 17.8 %collective-permute-start = (f32[64,2,8,128]{3,0,2,1:T(8,128)}, f32[64,2,8,128]{3,0,2,1:T(8,128)S(1)}, u32[]{:S(2)}, u32[]{:S(2)}) collective-permute-start(f32[64,2,8,128]{3,0,2,1:T(8,128)} %get-tuple-element.321), channel_id=1, source_target_pairs={{0,4},{4,8},{8,12},{12,16},{16,20},{20,24},{24,28},{28,0},{1,5},{5... | collective-permute-start | bytes 1572872 | tf_op jit(solution)/shard_map/while/body/eval_jaxpr/ppermute | solution.py:12
  63.7 21.6 %collective-permute-start.1 = (f32[2,8,64]{2,1,0:T(8,128)S(1)}, f32[2,8,64]{2,1,0:T(8,128)S(1)}, u32[]{:S(2)}, u32[]{:S(2)}) collective-permute-start(f32[2,8,64]{2,1,0:T(8,128)S(1)} %get-tuple-element.322), channel_id=1, source_target_pairs={{0,4},{4,8},{8,12},{12,16},{16,20},{20,24},{24,28},{28,0},{1,5},{5... | collective-permute-start | bytes 12296 | tf_op jit(solution)/shard_map/while/body/eval_jaxpr/ppermute | solution.py:12
  63.7 23.5 %collective-permute-start.2 = (f32[2,8,64]{2,1,0:T(8,128)S(1)}, f32[2,8,64]{2,1,0:T(8,128)S(1)}, u32[]{:S(2)}, u32[]{:S(2)}) collective-permute-start(f32[2,8,64]{2,1,0:T(8,128)S(1)} %get-tuple-element.323), channel_id=1, source_target_pairs={{0,4},{4,8},{8,12},{12,16},{16,20},{20,24},{24,28},{28,0},{1,5},{5... | collective-permute-start | bytes 12296 | tf_op jit(solution)/shard_map/while/body/eval_jaxpr/ppermute | solution.py:12
  63.8 27.1 %collective-permute-start.3 = (f32[64,2,8,128]{3,0,2,1:T(8,128)}, f32[64,2,8,128]{3,0,2,1:T(8,128)}, u32[]{:S(2)}, u32[]{:S(2)}) collective-permute-start(f32[64,2,8,128]{3,0,2,1:T(8,128)} %get-tuple-element.324), channel_id=1, source_target_pairs={{0,4},{4,8},{8,12},{12,16},{16,20},{20,24},{24,28},{28,0},{1,5},{5... | collective-permute-start | bytes 1572872 | tf_op jit(solution)/shard_map/while/body/eval_jaxpr/ppermute | solution.py:12
  81.5 9.3 %copy-start.2 = (f32[1024,2,128]{2,0,1:T(8,128)S(1)}, f32[1024,2,128]{2,0,1:T(8,128)}, u32[]{:S(2)}) copy-start(f32[1024,2,128]{2,0,1:T(8,128)} %get-tuple-element.339) | copy-start | bytes 3145732 | tf_op jit(solution)/shard_map/while
  98.4 32.6 %collective-permute-start.4 = (f32[64,2,8,128]{3,2,0,1:T(8,128)S(1)}, f32[64,2,8,128]{3,2,0,1:T(8,128)S(1)}, u32[]{:S(2)}, u32[]{:S(2)}) collective-permute-start(f32[64,2,8,128]{3,2,0,1:T(8,128)S(1)} %copy.37), channel_id=1, source_target_pairs={{0,24},{4,28},{8,0},{12,4},{16,8},{20,12},{24,16},{28,20},{1,25},{... | collective-permute-start | bytes 1572872 | tf_op jit(solution)/shard_map/ppermute | solution.py:12
  98.7 6.0 %copy-start.1 = (f32[1024,256]{0,1:T(8,128)S(1)}, f32[1024,256]{0,1:T(8,128)}, u32[]{:S(2)}) copy-start(f32[1024,256]{0,1:T(8,128)} %copy-done) | copy-start | bytes 3145732
  109.1 21.8 %collective-permute-start.8 = (f32[64,2,8,128]{3,2,0,1:T(8,128)S(1)}, f32[64,2,8,128]{3,2,0,1:T(8,128)S(1)}, u32[]{:S(2)}, u32[]{:S(2)}) collective-permute-start(f32[64,2,8,128]{3,2,0,1:T(8,128)S(1)} %fusion.56), channel_id=1, source_target_pairs={{0,4},{4,8},{8,12},{12,16},{16,20},{20,24},{24,28},{28,0},{1,5},{5... | collective-permute-start | bytes 1572872 | tf_op jit(solution)/shard_map/ppermute | solution.py:12
  109.4 5.5 %collective-permute-start.5 = (f32[2,8,64]{1,2,0:T(8,128)S(1)}, f32[2,8,64]{1,2,0:T(8,128)S(1)}, u32[]{:S(2)}, u32[]{:S(2)}) collective-permute-start(f32[2,8,64]{1,2,0:T(8,128)S(1)} %copy.38), channel_id=1, source_target_pairs={{0,24},{4,28},{8,0},{12,4},{16,8},{20,12},{24,16},{28,20},{1,25},{... | collective-permute-start | bytes 12296 | tf_op jit(solution)/shard_map/ppermute | solution.py:12
  109.5 17.6 %collective-permute-start.9 = (f32[2,8,64]{1,2,0:T(8,128)S(1)}, f32[2,8,64]{1,2,0:T(8,128)S(1)}, u32[]{:S(2)}, u32[]{:S(2)}) collective-permute-start(f32[2,8,64]{1,2,0:T(8,128)S(1)} %copy.42), channel_id=1, source_target_pairs={{0,24},{4,28},{8,0},{12,4},{16,8},{20,12},{24,16},{28,20},{1,25},{... | collective-permute-start | bytes 12296 | tf_op jit(solution)/shard_map/ppermute | solution.py:12
  109.6 18.9 %collective-permute-start.7 = (f32[2,8,64]{1,2,0:T(8,128)S(1)}, f32[2,8,64]{1,2,0:T(8,128)S(1)}, u32[]{:S(2)}, u32[]{:S(2)}) collective-permute-start(f32[2,8,64]{1,2,0:T(8,128)S(1)} %broadcast_maximum_fusion), channel_id=1, source_target_pairs={{0,4},{4,8},{8,12},{12,16},{16,20},{20,24},{24,28},{28,0},{1,5},{5... | collective-permute-start | bytes 12296 | tf_op jit(solution)/shard_map/ppermute | solution.py:12
  114.8 16.1 %collective-permute-start.10 = (f32[2,8,64]{1,2,0:T(8,128)S(1)}, f32[2,8,64]{1,2,0:T(8,128)S(1)}, u32[]{:S(2)}, u32[]{:S(2)}) collective-permute-start(f32[2,8,64]{1,2,0:T(8,128)S(1)} %get-tuple-element.237), channel_id=1, source_target_pairs={{0,4},{4,8},{8,12},{12,16},{16,20},{20,24},{24,28},{28,0},{1,5},{5... | collective-permute-start | bytes 12296 | tf_op jit(solution)/shard_map/ppermute | solution.py:12
where the time goes:
time: 133 us; the launch traced here: 132 us
  waiting for transfers between devices  42.1 us (32%)
  matrix products  40.3 us (30%)
  starting transfers between devices  28.1 us (21%)
  local copies, waits for them, and re-layouts  11.8 us (9%)
  other arithmetic  9.29 us (7%)
    ppermute x15, waiting for transfers between devices, passed_along(): lax.ppermute(shard, axis, [(i, (i + by) % size) for i in range(size)])  42.1 us
    ppermute x15, starting transfers between devices, passed_along(): lax.ppermute(shard, axis, [(i, (i + by) % size) for i in range(size)])  28.1 us
    dot_general x4, matrix products, attend(): jnp.einsum('hgqk,khd->qhgd', weights, value_tile, precision=lax.Precision...  22.6 us
    dot_general x4, matrix products, attend(): jnp.einsum('qhgd,khd->hgqk', query_tile, key_tile, precision=lax.Precisio...  17.7 us
    unnamed x14, local copies, waits for them, and re-layouts  7.77 us
    reduce_sum x4, other arithmetic, attend(): weight_sum = weight_sum * factor + jnp.sum(weights, axis=-1)  6.28 us
  transfers between devices with their start and end apart: 15, of which 6 were waited for; matrix products, arithmetic and copies ran while one was open for 44% of the time, Pallas kernels for 0%

commit v1 on v0

--- a/solution.py
+++ b/solution.py
@@ -1,10 +1,347 @@
+import functools
+import math
+
 import jax
 import jax.numpy as jnp
 from jax import lax
+from jax.experimental import pallas as pl
+from jax.experimental.pallas import tpu as pltpu
 from jax.sharding import PartitionSpec as P
 
 HEAD_DIM = 128
 SPAN = 6
+CH = 4
+MESH = pl.DeviceIdType.MESH
+F32 = jnp.float32
+BF16 = jnp.bfloat16
+
+
+def split2(a):
+    hi = a.astype(BF16)
+    return hi, (a - hi.astype(F32)).astype(BF16)
+
+
+def pair_kernel(
+    blocks, group, n_ref, q_hbm, k_hbm, v_hbm, out_ref,
+    kraw, vraw, ka, kb, va, q_own, qx, qz, qf,
+    own_num, own_st, loc_num, loc_st,
+    px_s, pz_s, pf_s, px_r, pz_r, pf_r,
+    lsem, q_ss, q_rs, p_ss, p_rs,
+):
+    b = lax.axis_index("blk")
+    x = lax.rem(b, 2)
+    rows = q_own.shape[0]
+    keys = kraw.shape[0]
+    kv = kraw.shape[1] // HEAD_DIM
+    chunks = q_own.shape[1] // (CH * HEAD_DIM)
+    tb = rows // 8
+    partner = b + 1 - 2 * x
+    up, down = b + 2, b - 2
+    has_up, has_down = up < blocks, down >= 0
+    fdst, fsrc = b + 2 - 4 * x, b - 2 + 4 * x
+    has_fdst = (fdst >= 0) & (fdst < blocks)
+    has_fsrc = (fsrc >= 0) & (fsrc < blocks)
+
+    barrier = pltpu.get_barrier_semaphore()
+    pl.semaphore_signal(barrier, inc=1, device_id={"blk": partner}, device_id_type=MESH)
+
+    @pl.when(has_up)
+    def _():
+        pl.semaphore_signal(barrier, inc=1, device_id={"blk": up}, device_id_type=MESH)
+
+    @pl.when(has_down)
+    def _():
+        pl.semaphore_signal(barrier, inc=1, device_id={"blk": down}, device_id_type=MESH)
+
+    own_copy = pltpu.make_async_copy(q_hbm, q_own, lsem.at[0])
+    k_copy = pltpu.make_async_copy(k_hbm, kraw, lsem.at[1])
+    v_copy = pltpu.make_async_copy(v_hbm, vraw, lsem.at[2])
+    k_copy.start()
+    v_copy.start()
+    own_copy.start()
+    pl.semaphore_wait(
+        barrier, 1 + jnp.where(has_up, 1, 0) + jnp.where(has_down, 1, 0)
+    )
+
+    def cols(c):
+        return pl.ds(pl.multiple_of(c * (CH * HEAD_DIM), CH * HEAD_DIM), CH * HEAD_DIM)
+
+    def qcopy(kind, src, dst, c, to):
+        return pltpu.make_async_remote_copy(
+            src_ref=src.at[:, cols(c)], dst_ref=dst.at[:, cols(c)],
+            send_sem=q_ss.at[kind, c], recv_sem=q_rs.at[kind, c],
+            device_id={"blk": to}, device_id_type=MESH,
+        )
+
+    def x_copy(c):
+        return qcopy(0, q_hbm, qx, c, partner)
+
+    def z_copy(c):
+        return qcopy(1, q_hbm, qz, c, up)
+
+    def f_copy(c):
+        return qcopy(2, qx, qf, c, fdst)
+
+    def pcopy(kind, src, dst, c, to):
+        return pltpu.make_async_remote_copy(
+            src_ref=src.at[c], dst_ref=dst.at[c],
+            send_sem=p_ss.at[kind, c], recv_sem=p_rs.at[kind, c],
+            device_id={"blk": to}, device_id_type=MESH,
+        )
+
+    def px_copy(c):
+        return pcopy(0, px_s, px_r, c, partner)
+
+    def pz_copy(c):
+        return pcopy(1, pz_s, pz_r, c, down)
+
+    def pf_copy(c):
+        return pcopy(2, pf_s, pf_r, c, fsrc)
+
+    def start_x(c, carry):
+        x_copy(c).start()
+        return carry
+
+    lax.fori_loop(0, chunks, start_x, 0)
+
+    @pl.when(has_up)
+    def _():
+        z_copy(0).start()
+
+    lane = lax.broadcasted_iota(jnp.int32, (rows, HEAD_DIM), 1)
+    valid = n_ref[0]
+    klane = lax.broadcasted_iota(jnp.int32, (keys, HEAD_DIM), 1)
+    krow = lax.broadcasted_iota(jnp.int32, (keys, HEAD_DIM), 0)
+    bias = jnp.where((klane == 0) & (krow >= valid), -1e30, 0.0).astype(BF16)
+    k_copy.wait()
+    for g in range(kv):
+        hi, lo = split2(kraw[:, g * HEAD_DIM:(g + 1) * HEAD_DIM])
+        ka[g, :, :HEAD_DIM] = hi
+        ka[g, :, HEAD_DIM:] = hi
+        kb[g, :, :HEAD_DIM] = lo
+        kb[g, :, HEAD_DIM:] = bias
+    v_copy.wait()
+    for g in range(kv):
+        hi, lo = split2(vraw[:, g * HEAD_DIM:(g + 1) * HEAD_DIM])
+        va[g, :, :HEAD_DIM] = hi
+        va[g, :, HEAD_DIM:] = lo
+    own_copy.wait()
+
+    qlane = lax.broadcasted_iota(jnp.int32, (CH * rows, HEAD_DIM), 1)
+    one = jnp.where(qlane == 0, 1.0, 0.0).astype(BF16)
+    scale = HEAD_DIM ** (-0.5) * math.log2(math.e)
+
+    def attend(q_ref, c):
+        g = (c * CH) // group
+        q = q_ref[:, cols(c)]
+        q = jnp.concatenate(
+            [q[:, h * HEAD_DIM:(h + 1) * HEAD_DIM] for h in range(CH)], axis=0
+        ) * scale
+        hi, lo = split2(q)
+        dims = (((1,), (1,)), ((), ()))
+        s = lax.dot_general(
+            jnp.concatenate([hi, lo], axis=1), ka[g], dims, preferred_element_type=F32
+        ) + lax.dot_general(
+            jnp.concatenate([hi, one], axis=1), kb[g], dims, preferred_element_type=F32
+        )
+        m = jnp.max(s, axis=1, keepdims=True)
+        p = jnp.exp2(s - m)
+        l = jnp.sum(p, axis=1, keepdims=True)
+        p_hi, p_lo = split2(p)
+        r = jnp.dot(p_hi, va[g], preferred_element_type=F32)
+        num = r[:, :HEAD_DIM] + r[:, HEAD_DIM:] + jnp.dot(
+            p_lo, va[g, :, :HEAD_DIM], preferred_element_type=F32
+        )
+        st = jnp.zeros((rows, HEAD_DIM), F32)
+        for h in range(CH):
+            st = jnp.where(lane == h, m[h * rows:(h + 1) * rows], st)
+            st = jnp.where(lane == CH + h, l[h * rows:(h + 1) * rows], st)
+        return num, st
+
+    def pack(buf, c, num, st):
+        buf[c, :CH * tb] = num.reshape(CH * tb, 8, HEAD_DIM)
+        wide = jnp.concatenate([st] * (HEAD_DIM // rows), axis=0)
+        buf[c, CH * tb] = wide.T[:8]
+
+    def unpack(buf, c):
+        num = buf[c, :CH * tb].reshape(CH * rows, HEAD_DIM)
+        st = jnp.concatenate([buf[c, CH * tb]] * (HEAD_DIM // 8), axis=0).T[:rows]
+        return num, st
+
+    def column(st, h):
+        return st[:, h:h + 1]
+
+    def merge(a, o):
+        top = jnp.maximum(a[1], o[1])
+        fa, fo = jnp.exp2(a[1] - top), jnp.exp2(o[1] - top)
+        total = a[1] * pltpu.roll(fa, CH, 1) + o[1] * pltpu.roll(fo, CH, 1)
+        st = jnp.where(lane < CH, top, total)
+        parts = []
+        for h in range(CH):
+            part = slice(h * rows, (h + 1) * rows)
+            parts.append(a[0][part] * column(fa, h) + o[0][part] * column(fo, h))
+        return jnp.concatenate(parts, axis=0), st
+
+    def step(t, carry):
+        early = t < chunks
+        zc = jnp.where(t == 0, 0, t - chunks)
+        late = (t == 0) | ((t > chunks) & (zc < chunks))
+
+        @pl.when(late)
+        def _():
+            num, st = attend(q_own, zc)
+            own_num[zc] = num
+            own_st[zc] = st
+
+        @pl.when(early)
+        def _():
+            x_copy(t).wait_recv()
+
+            @pl.when(has_fdst)
+            def _():
+                f_copy(t).start()
+
+            num, st = attend(qx, t)
+            loc_num[t] = num
+            loc_st[t] = st
+
+        @pl.when((t == chunks - 1) & has_up)
+        def _():
+            def start_z(c, carry):
+                z_copy(c).start()
+                return carry
+
+            lax.fori_loop(1, chunks, start_z, 0)
+
+        @pl.when(late & has_down)
+        def _():
+            z_copy(zc).wait_recv()
+            num, st = attend(qz, zc)
+            pack(pz_s, zc, num, st)
+            pz_copy(zc).start()
+
+        fc = t - 1
+
+        @pl.when((fc >= 0) & (fc < chunks) & has_fsrc)
+        def _():
+            f_copy(fc).wait_recv()
+            num, st = attend(qf, fc)
+            pack(pf_s, fc, num, st)
+            pf_copy(fc).start()
+
+        mc = t - 2
+
+        @pl.when((mc >= 0) & (mc < chunks))
+        def _():
+            @pl.when(has_fdst)
+            def _():
+                pf_copy(mc).wait_recv()
+                num, st = merge((loc_num[mc], loc_st[mc]), unpack(pf_r, mc))
+                pack(px_s, mc, num, st)
+
+            @pl.when(jnp.logical_not(has_fdst))
+            def _():
+                pack(px_s, mc, loc_num[mc], loc_st[mc])
+
+            px_copy(mc).start()
+
+        return carry
+
+    lax.fori_loop(0, 2 * chunks, step, 0)
+
+    def finish(c, carry):
+        px_copy(c).wait_recv()
+        num, st = merge((own_num[c], own_st[c]), unpack(px_r, c))
+        own_num[c] = num
+        own_st[c] = st
+
+        @pl.when(has_up)
+        def _():
+            pz_copy(c).wait_recv()
+            num, st = merge((own_num[c], own_st[c]), unpack(pz_r, c))
+            own_num[c] = num
+            own_st[c] = st
+
+        st = own_st[c]
+        num = own_num[c]
+        out_ref[:, cols(c)] = jnp.concatenate(
+            [num[h * rows:(h + 1) * rows] / column(st, CH + h) for h in range(CH)], axis=1
+        )
+        return carry
+
+    lax.fori_loop(0, chunks, finish, 0)
+
+    def drain(c, carry):
+        x_copy(c).wait_send()
+        px_copy(c).wait_send()
+
+        @pl.when(has_up)
+        def _():
+            z_copy(c).wait_send()
+
+        @pl.when(has_down)
+        def _():
+            pz_copy(c).wait_send()
+
+        @pl.when(has_fdst)
+        def _():
+            f_copy(c).wait_send()
+
+        @pl.when(has_fsrc)
+        def _():
+            pf_copy(c).wait_send()
+
+        return carry
+
+    lax.fori_loop(0, chunks, drain, 0)
+
+
+def paired(queries, visual_keys, projected_values, valid_lengths):
+    blocks = lax.axis_size("blk")
+    rows, width = queries.shape
+    keys, kv_width = visual_keys.shape
+    kv = kv_width // HEAD_DIM
+    group = width // kv_width
+    chunks = width // (CH * HEAD_DIM)
+    tiles = CH * rows // 8 + 1
+    vmem = pltpu.VMEM
+    part = vmem((chunks, tiles, 8, HEAD_DIM), F32)
+    any_spec = pl.BlockSpec(memory_space=pl.ANY)
+    pairs = 4 * rows * (width // HEAD_DIM) * keys
+    return pl.pallas_call(
+        functools.partial(pair_kernel, blocks, group),
+        out_shape=jax.ShapeDtypeStruct((rows, width), F32),
+        in_specs=[pl.BlockSpec(memory_space=pltpu.SMEM), any_spec, any_spec, any_spec],
+        out_specs=pl.BlockSpec(memory_space=vmem),
+        scratch_shapes=[
+            vmem((keys, kv_width), F32),
+            vmem((keys, kv_width), F32),
+            vmem((kv, keys, 2 * HEAD_DIM), BF16),
+            vmem((kv, keys, 2 * HEAD_DIM), BF16),
+            vmem((kv, keys, 2 * HEAD_DIM), BF16),
+            vmem((rows, width), F32),
+            vmem((rows, width), F32),
+            vmem((rows, width), F32),
+            vmem((rows, width), F32),
+            vmem((chunks, CH * rows, HEAD_DIM), F32),
+            vmem((chunks, rows, HEAD_DIM), F32),
+            vmem((chunks, CH * rows, HEAD_DIM), F32),
+            vmem((chunks, rows, HEAD_DIM), F32),
+            part, part, part, part, part, part,
+            pltpu.SemaphoreType.DMA((3,)),
+            pltpu.SemaphoreType.DMA((3, chunks)),
+            pltpu.SemaphoreType.DMA((3, chunks)),
+            pltpu.SemaphoreType.DMA((3, chunks)),
+            pltpu.SemaphoreType.DMA((3, chunks)),
+        ],
+        compiler_params=pltpu.CompilerParams(
+            collective_id=0, has_side_effects=True, vmem_limit_bytes=44 * 1024 * 1024
+        ),
+        cost_estimate=pl.CostEstimate(
+            flops=pairs * HEAD_DIM * 4, bytes_accessed=4 * (2 * rows * width + 2 * keys * kv_width),
+            transcendentals=pairs,
+        ),
+    )(valid_lengths, queries, visual_keys, projected_values)
 
 
 def passed_along(shard, axis, by):
@@ -106,8 +443,10 @@
 
 
 def solution(mesh):
+    blocks = mesh.shape["blk"]
+    body = paired if blocks % 2 == 0 and min(SPAN, blocks // 2) == 4 else per_device
     return jax.shard_map(
-        per_device,
+        body,
         mesh=mesh,
         in_specs=(P("blk", "heads"), P("blk", "heads"), P("blk", "heads"), P("blk")),
         out_specs=P("blk", "heads"),

time: 133 us -> 49.5 us (0.37)
  the two profiles are of different devices: /device:TPU:0 before, /device:TPU:10 now
where the time goes in v1:
time: 49.5 us; the launch traced here: 49.2 us
  Pallas kernels  44.3 us (89%)
  local copies, waits for them, and re-layouts  4.28 us (9%)
  between operations  0.67 us (1%)
    pallas_call x1, Pallas kernels, paired(): pl.pallas_call(functools.partial(pair_kernel, blocks, group), out_shape=j...  44.3 us
    unnamed x7, local copies, waits for them, and re-layouts  4.28 us

profile of v1, /device:TPU:10, one launch (start us, length us, event | category | flops | bytes accessed | tf_op | source)
XLA Modules:
  0.0 49.2 jit_solution(8582415838341896925)
XLA Ops:
  0.7 0.0 copy-start
  0.7 1.2 %copy-done = f32[1024,256]{1,0:T(8,128)S(1)} copy-done((f32[1024,256]{1,0:T(8,128)S(1)}, f32[1024,256]{1,0:T(8,128)}, u32[]{:S(2)}) %copy-start) | copy-done | bytes 1048600
  1.9 0.0 copy-start.1
  1.9 1.2 %copy-done.1 = f32[1024,256]{1,0:T(8,128)S(1)} copy-done((f32[1024,256]{1,0:T(8,128)S(1)}, f32[1024,256]{1,0:T(8,128)}, u32[]{:S(2)}) %copy-start.1) | copy-done | bytes 1048600
  3.1 0.0 copy-start.2
  3.1 1.0 %copy-done.2 = f32[64,2048]{1,0:T(8,128)S(1)} copy-done((f32[64,2048]{1,0:T(8,128)S(1)}, f32[64,2048]{1,0:T(8,128)}, u32[]{:S(2)}) %copy-start.2) | copy-done | bytes 524312
  4.1 44.3 %shard_map.46 = f32[64,2048]{1,0:T(8,128)S(1)} custom-call(s32[1]{0:T(128)S(6)} %copy.6.n_ref, f32[64,2048]{1,0:T(8,128)S(1)} %copy-done.2, f32[1024,256]{1,0:T(8,128)S(1)} %copy-done, f32[1024,256]{1,0:T(8,128)S(1)} %copy-done.1), custom_call_target="tpu_custom_call" | custom-call | flops 2147483648 | bytes 3145728 | tf_op jit(solution)/shard_map/pallas_call | solution.py:311
  48.4 0.8 %copy.7 = f32[64,2048]{1,0:T(8,128)} copy(f32[64,2048]{1,0:T(8,128)S(1)} %shard_map.46) | data formatting | bytes 1048576
Async XLA Ops:
  0.7 1.2 %copy-start = (f32[1024,256]{1,0:T(8,128)S(1)}, f32[1024,256]{1,0:T(8,128)}, u32[]{:S(2)}) copy-start(f32[1024,256]{1,0:T(8,128)} %k_hbm.1) | copy-start | bytes 3145732
  1.9 1.2 %copy-start.1 = (f32[1024,256]{1,0:T(8,128)S(1)}, f32[1024,256]{1,0:T(8,128)}, u32[]{:S(2)}) copy-start(f32[1024,256]{1,0:T(8,128)} %v_hbm.1) | copy-start | bytes 3145732
  3.1 1.0 %copy-start.2 = (f32[64,2048]{1,0:T(8,128)S(1)}, f32[64,2048]{1,0:T(8,128)}, u32[]{:S(2)}) copy-start(f32[64,2048]{1,0:T(8,128)} %q_hbm.1) | copy-start | bytes 1572868

commit v2 on v1

--- a/solution.py
+++ b/solution.py
@@ -11,6 +11,9 @@
 HEAD_DIM = 128
 SPAN = 6
 CH = 4
+AHEAD = 2
+EARLY = 2
+SKEW = 2
 MESH = pl.DeviceIdType.MESH
 F32 = jnp.float32
 BF16 = jnp.bfloat16
@@ -102,11 +105,17 @@
         x_copy(c).start()
         return carry
 
-    lax.fori_loop(0, chunks, start_x, 0)
+    lax.fori_loop(0, min(AHEAD, chunks), start_x, 0)
+
+    early = min(EARLY, chunks)
+
+    def start_z(c, carry):
+        z_copy(c).start()
+        return carry
 
     @pl.when(has_up)
     def _():
-        z_copy(0).start()
+        lax.fori_loop(0, early, start_z, 0)
 
     lane = lax.broadcasted_iota(jnp.int32, (rows, HEAD_DIM), 1)
     valid = n_ref[0]
@@ -183,17 +192,25 @@
         return jnp.concatenate(parts, axis=0), st
 
     def step(t, carry):
-        early = t < chunks
-        zc = jnp.where(t == 0, 0, t - chunks)
-        late = (t == 0) | ((t > chunks) & (zc < chunks))
-
-        @pl.when(late)
+        zc = jnp.where(t < early, t, t - chunks)
+        use_z = (t < early) | ((zc >= early) & (zc < chunks))
+        fc = t - SKEW
+        use_f = (fc >= 0) & (fc < chunks)
+        mc = t - 2 * SKEW
+
+        @pl.when(use_z)
         def _():
             num, st = attend(q_own, zc)
             own_num[zc] = num
             own_st[zc] = st
 
-        @pl.when(early)
+        @pl.when(use_f)
+        def _():
+            num, st = attend(qx, fc)
+            loc_num[fc] = num
+            loc_st[fc] = st
+
+        @pl.when(t < chunks)
         def _():
             x_copy(t).wait_recv()
 
@@ -201,35 +218,29 @@
             def _():
                 f_copy(t).start()
 
-            num, st = attend(qx, t)
-            loc_num[t] = num
-            loc_st[t] = st
+            x_copy(t).wait_send()
+
+            @pl.when(t + AHEAD < chunks)
+            def _():
+                x_copy(t + AHEAD).start()
 
         @pl.when((t == chunks - 1) & has_up)
         def _():
-            def start_z(c, carry):
-                z_copy(c).start()
-                return carry
-
-            lax.fori_loop(1, chunks, start_z, 0)
-
-        @pl.when(late & has_down)
+            lax.fori_loop(early, chunks, start_z, 0)
+
+        @pl.when(use_z & has_down)
         def _():
             z_copy(zc).wait_recv()
             num, st = attend(qz, zc)
             pack(pz_s, zc, num, st)
             pz_copy(zc).start()
 
-        fc = t - 1
-
-        @pl.when((fc >= 0) & (fc < chunks) & has_fsrc)
+        @pl.when(use_f & has_fsrc)
         def _():
             f_copy(fc).wait_recv()
             num, st = attend(qf, fc)
             pack(pf_s, fc, num, st)
             pf_copy(fc).start()
-
-        mc = t - 2
 
         @pl.when((mc >= 0) & (mc < chunks))
         def _():
@@ -247,7 +258,7 @@
 
         return carry
 
-    lax.fori_loop(0, 2 * chunks, step, 0)
+    lax.fori_loop(0, max(2 * chunks, chunks + 2 * SKEW), step, 0)
 
     def finish(c, carry):
         px_copy(c).wait_recv()
@@ -272,7 +283,6 @@
     lax.fori_loop(0, chunks, finish, 0)
 
     def drain(c, carry):
-        x_copy(c).wait_send()
         px_copy(c).wait_send()
 
         @pl.when(has_up)
@@ -335,7 +345,7 @@
             pltpu.SemaphoreType.DMA((3, chunks)),
         ],
         compiler_params=pltpu.CompilerParams(
-            collective_id=0, has_side_effects=True, vmem_limit_bytes=44 * 1024 * 1024
+            collective_id=0, has_side_effects=True, vmem_limit_bytes=62 * 1024 * 1024
         ),
         cost_estimate=pl.CostEstimate(
             flops=pairs * HEAD_DIM * 4, bytes_accessed=4 * (2 * rows * width + 2 * keys * kv_width),

time: 49.5 us -> 41 us (0.83)
  the two profiles are of different devices: /device:TPU:10 before, /device:TPU:0 now
where the time goes in v2:
time: 41 us; the launch traced here: 40.6 us
  Pallas kernels  38.1 us (93%)
  local copies, waits for them, and re-layouts  1.87 us (5%)
  between operations  0.66 us (2%)
    pallas_call x1, Pallas kernels, paired(): pl.pallas_call(functools.partial(pair_kernel, blocks, group), out_shape=j...  38.1 us
    unnamed x1, local copies, waits for them, and re-layouts  1.87 us

profile of v2, /device:TPU:0, one launch (start us, length us, event | category | flops | bytes accessed | tf_op | source)
XLA Modules:
  0.0 40.6 jit_solution(1357950293759000784)
XLA Ops:
  0.7 38.1 %shard_map.46 = f32[64,2048]{1,0:T(8,128)} custom-call(s32[1]{0:T(128)S(6)} %copy.6.n_ref, f32[64,2048]{1,0:T(8,128)} %q_hbm.1, f32[1024,256]{1,0:T(8,128)} %k_hbm.1, f32[1024,256]{1,0:T(8,128)} %v_hbm.1), custom_call_target="tpu_custom_call" | custom-call | flops 2147483648 | bytes 3145728 | tf_op jit(solution)/shard_map/pallas_call | solution.py:321
  38.7 1.9 %copy.7 = f32[64,2048]{1,0:T(8,128)} copy(f32[64,2048]{1,0:T(8,128)} %shard_map.46) | data formatting | bytes 1048576
